TPU v7x, 32 devices: a whole 2x2x4 slice. The times are simulated.
32 devices in a mesh: groups: 1, clus: 8 (over z, core), sub: 4 (over y, x).
Axes of the slice: x: 2, y: 2, z: 4, core: 2. Of those that a mesh axis runs over, the one named last changes fastest.
Arguments:
- loads: bfloat16 [12, 3, 65536], P(None, None, ('groups', 'clus', 'sub')), may hold values from -6 to 6
- centers: bfloat16 [3, 65536], P(None, ('groups', 'clus', 'sub'))
- basis: bfloat16 [256, 96, 3, 256], P(('groups', 'clus', 'sub')), may hold values from -0.625 to 0.625
- up_leaf: bfloat16 [256, 96, 96], P(('groups', 'clus', 'sub')), may hold values from -0.625 to 0.625
- up_mid: bfloat16 [128, 96, 96], P(('groups', 'clus', 'sub')), may hold values from -0.625 to 0.625
- up_top: bfloat16 [64, 96, 96], P(('groups', 'clus', 'sub')), may hold values from -0.625 to 0.625
- couplings: bfloat16 [480, 12, 96, 96], P(('groups', 'clus', 'sub')), may hold values from -0.046875 to 0.046875
- far_dest: int32 [480, 12], P(('groups', 'clus', 'sub')), may hold values from 0 to 31, all different within a row; in each aligned block of 15 rows (0 to 14, 15 to 29, ...) at most 6 rows name the same one
- far_target: int32 [480, 12], P(('groups', 'clus', 'sub')), may hold values from 0 to 7, as said below
- near_src: int32 [256, 6], P(('groups', 'clus', 'sub')), may hold values from 0 to 255, as said below
Outputs:
- field: float32 [12, 3, 65536], P(None, None, ('groups', 'clus', 'sub'))
Inputs may be any that keep to these rules, and one draw needn't show every extreme that they name: `far_dest`: the rows of one device (aligned blocks of 15 rows) name one device at most 6 times in all, some device exactly so; a row names 12 different devices. far_target[r, k] is below the number of clusters a device holds at the level of row r: 8, 4, 2 or 1. `near_src`: row t starts with t; its other entries differ from t and lie at most 8 leaves from t, some exactly 8.
All inputs are finite; a program needn't handle non-finite values.
Results may differ from a plain program's by a relative error of at most 0.0095.
Values may be sent and summed in bfloat16 or wider, within the bound.
A program may use at most 64 MiB of HBM per device.

v0:
```python
import math

import jax
import jax.numpy as jnp
from jax import lax
from jax.sharding import PartitionSpec as P

CORE_SQ = 0.0625
KELVIN = 1.0 / (16.0 * math.pi * 0.7)
SHEAR = 1.8


def padded(block, sides, width):
    for axis, dim in sides:
        count = lax.axis_size(axis)
        forward = [(i, i + 1) for i in range(count - 1)]
        backward = [(target, source) for source, target in forward]
        low = lax.ppermute(
            lax.slice_in_dim(block, block.shape[dim] - width, None, axis=dim), axis, forward
        )
        high = lax.ppermute(lax.slice_in_dim(block, 0, width, axis=dim), axis, backward)
        block = jnp.concatenate([low, block, high], axis=dim)
    return block


def kelvin_tile(target_pts, source_pts):
    diff = target_pts[None, :, :, None] - source_pts[:, :, None, :]
    dist_sq = jnp.sum(diff * diff, axis=1) + CORE_SQ
    scale = KELVIN * lax.rsqrt(dist_sq)
    inverse = 1.0 / dist_sq
    outer = diff[:, :, None] * diff[:, None, :] * inverse[:, None, None]
    eye_block = jnp.eye(3, dtype=jnp.float32)[None, :, :, None, None]
    return ((SHEAR * eye_block + outer) * scale[:, None, None]).astype(jnp.bfloat16)


def climb(weights, child):
    prod = jnp.einsum("kab,kbc->kac", weights, child, preferred_element_type=jnp.float32)
    prod = prod.reshape(prod.shape[0] // 2, 2, prod.shape[1], prod.shape[2])
    return (prod[:, 0] + prod[:, 1]).astype(jnp.bfloat16)


def descend(weights, incoming, parent):
    spread = jnp.repeat(parent, 2, axis=0)
    moved = jnp.einsum("kab,kac->kbc", weights, spread, preferred_element_type=jnp.float32)
    return (incoming + moved).astype(jnp.bfloat16)


def pack_slots(products, dests, targets, ndev, cap):
    hits = (dests[:, None] == jnp.arange(ndev, dtype=jnp.int32)[None, :]).astype(jnp.int32)
    before = jnp.cumsum(hits, axis=0) - hits
    slot = dests * cap + jnp.sum(before * hits, axis=1)
    buffer = jnp.zeros((ndev * cap, products.shape[1]), jnp.bfloat16).at[slot].set(products)
    labels = jnp.full((ndev * cap,), -1, jnp.int32).at[slot].set(targets)
    return (buffer, labels)


def collect(got, tags, count):
    width = got.shape[-1]
    tags = tags.reshape(-1)
    got = got.reshape(-1, width)
    pick = (tags[:, None] == jnp.arange(count, dtype=jnp.int32)[None, :]).astype(jnp.bfloat16)
    return jnp.einsum("sq,sw->qw", pick, got, preferred_element_type=jnp.float32)


def level_route(products, dests, targets, count, nclus, nsub, cap):
    buffer, labels = pack_slots(products, dests, targets, nclus * nsub, cap)
    buffer = buffer.reshape(nclus, nsub, cap, products.shape[1])
    labels = labels.reshape(nclus, nsub, cap)
    got, tags = (
        lax.all_to_all(
            lax.all_to_all(buffer, "clus", split_axis=0, concat_axis=0, tiled=True),
            "sub",
            split_axis=1,
            concat_axis=1,
            tiled=True,
        ),
        lax.all_to_all(
            lax.all_to_all(labels, "clus", split_axis=0, concat_axis=0, tiled=True),
            "sub",
            split_axis=1,
            concat_axis=1,
            tiled=True,
        ),
    )
    return collect(got, tags, count)


def body(loads, centers, basis, up_leaf, up_mid, up_top, couplings, far_dest, far_target, near_src):
    cases = loads.shape[0]
    per_dev, rank3, _, leaf = basis.shape
    nclus = lax.axis_size("clus")
    nsub = lax.axis_size("sub")
    ndev = nclus * nsub
    per_row = 2 * per_dev - 1
    fan = far_dest.shape[1]
    cap = max(2, (per_row * fan + ndev - 1) // ndev)
    width = rank3 * cases
    blocks = loads.reshape(cases, 3, per_dev, leaf)
    coef_leaf = jnp.einsum(
        "trip,citp->trc", basis, blocks, preferred_element_type=jnp.float32
    ).astype(jnp.bfloat16)
    coef_mid = climb(up_leaf, coef_leaf)
    coef_high = climb(up_mid, coef_mid)
    coef_top = climb(up_top, coef_high)
    coef_all = jnp.concatenate([coef_leaf, coef_mid, coef_high, coef_top], axis=0)
    contrib = jnp.einsum(
        "rkab,rbc->rkac", couplings, coef_all, preferred_element_type=jnp.float32
    ).astype(jnp.bfloat16)
    starts = [0, per_dev, per_dev + per_dev // 2, per_dev + per_dev // 2 + per_dev // 4, per_row]
    pieces = []
    for level in range(4):
        lower = starts[level]
        upper = starts[level + 1]
        level_cap = min(cap, upper - lower)
        pieces.append(
            level_route(
                contrib[lower:upper].reshape(-1, width),
                far_dest[lower:upper].reshape(-1),
                far_target[lower:upper].reshape(-1),
                upper - lower,
                nclus,
                nsub,
                level_cap,
            )
        )
    incoming = jnp.concatenate(pieces, axis=0)
    incoming = incoming.reshape(per_row, rank3, cases)
    w_top = incoming[starts[3] :].astype(jnp.bfloat16)
    w_high = descend(up_top, incoming[starts[2] : starts[3]], w_top)
    w_mid = descend(up_mid, incoming[starts[1] : starts[2]], w_high)
    w_leaf = descend(up_leaf, incoming[: starts[1]], w_mid)
    far = jnp.einsum("trip,trc->citp", basis, w_leaf, preferred_element_type=jnp.float32)
    window, shell = (
        padded(loads, ((("clus", "sub"), 2),), per_dev * leaf),
        padded(centers.reshape(1, 3, -1), ((("clus", "sub"), 2),), per_dev * leaf),
    )
    base = lax.axis_index(("clus", "sub")) * per_dev - per_dev
    local = near_src - base
    win_blocks = window.reshape(cases, 3, 3 * per_dev, leaf)
    win_pts = shell.reshape(3, 3 * per_dev, leaf).astype(jnp.float32)
    own_pts = centers.astype(jnp.float32).reshape(3, per_dev, leaf)

    def one_leaf(index):
        srcs = local[index]
        src_pts = jnp.transpose(win_pts[:, srcs], (1, 0, 2))
        tile = kelvin_tile(own_pts[:, index], src_pts)
        src_loads = win_blocks[:, :, srcs]
        return jnp.einsum("kijpq,cjkq->cip", tile, src_loads, preferred_element_type=jnp.float32)

    near = lax.map(one_leaf, jnp.arange(per_dev, dtype=jnp.int32))
    near = jnp.transpose(near, (1, 2, 0, 3))
    return (far + near).reshape(cases, 3, per_dev * leaf)


def solution(mesh):
    return jax.shard_map(
        body,
        mesh=mesh,
        in_specs=(
            P(None, None, ("groups", "clus", "sub")),
            P(None, ("groups", "clus", "sub")),
            P(("groups", "clus", "sub"), None, None, None),
            P(("groups", "clus", "sub"), None, None),
            P(("groups", "clus", "sub"), None, None),
            P(("groups", "clus", "sub"), None, None),
            P(("groups", "clus", "sub"), None, None, None),
            P(("groups", "clus", "sub"), None),
            P(("groups", "clus", "sub"), None),
            P(("groups", "clus", "sub"), None),
        ),
        out_specs=P(None, None, ("groups", "clus", "sub")),
        check_vma=False,
    )
```

profile of v0, /device:TPU:0, one launch (start us, length us, event | category | flops | bytes accessed | tf_op | source)
XLA Modules:
  0.0 336.2 jit_solution(2851667994990901867)
XLA Ops:
  3.8 6.3 %all-to-all-start.12 = ((s32[8,4,1]{1,2,0:T(1,128)}), s32[8,4,1]{1,2,0:T(1,128)S(1)}, u32[]{:S(2)}, u32[]{:S(2)}) async-start(s32[8,4,1]{1,2,0:T(1,128)} %bitcast.43), calls=%async_computation.12 | async-start | bytes 8192 | tf_op jit(solution)/shard_map/all_to_all | solution.py:78
  26.1 5.1 %all-to-all-start.8 = ((s32[8,4,2]{1,2,0:T(2,128)}), s32[8,4,2]{1,2,0:T(2,128)S(1)}, u32[]{:S(2)}, u32[]{:S(2)}) async-start(s32[8,4,2]{1,2,0:T(2,128)} %copy.193), calls=%async_computation.8 | async-start | bytes 16384 | tf_op jit(solution)/shard_map/all_to_all | solution.py:78
  41.0 4.7 %all-to-all-done.4 = s32[8,4,4]{2,1,0:T(4,128)S(1)} async-done(((s32[8,4,4]{2,1,0:T(4,128)}), s32[8,4,4]{2,1,0:T(4,128)S(1)}, u32[]{:S(2)}, u32[]{:S(2)}) %all-to-all-start.4) | async-done | bytes 544 | tf_op jit(solution)/shard_map/all_to_all | solution.py:78
  65.5 5.0 %fusion.7 = bf16[15,12,96,12]{2,3,1,0:T(8,128)(2,1)S(1)} fusion(bf16[15,12,96,96]{3,2,1,0:T(8,128)(2,1)} %param.18, bf16[1,96,12]{1,2,0:T(8,128)(2,1)S(1)} %fusion.44, bf16[2,96,12]{1,2,0:T(8,128)(2,1)S(1)} %fusion.39, bf16[4,96,12]{1,2,0:T(8,128)(2,1)S(1)} %fusion.36, bf16[8,96,12]{1,2,0:T(8,128)(2,1)S(1)} %fusion.9), kind=kOutput, calls=%fused_computation.29 | convolution fusion | flops 40158720 | bytes 3767040 | tf_op jit(solution)/shard_map/rkab,rbc->rkac/dot_general | solution.py:106
  72.5 5.0 %all-to-all-start.14 = ((bf16[8,4,1,1152]{3,1,2,0:T(4,128)(2,1)}), bf16[8,4,1,1152]{3,1,2,0:T(4,128)(2,1)S(1)}, u32[]{:S(2)}, u32[]{:S(2)}) async-start(bf16[8,4,1,1152]{3,1,2,0:T(4,128)(2,1)} %bitcast.44), calls=%async_computation.14 | async-start | bytes 147456 | tf_op jit(solution)/shard_map/all_to_all | solution.py:71
  78.8 5.2 %collective-permute-start = (bf16[12,3,2048]{2,1,0:T(4,128)(2,1)}, bf16[12,3,2048]{2,1,0:T(4,128)(2,1)}, u32[]{:S(2)}, u32[]{:S(2)}) collective-permute-start(bf16[12,3,2048]{2,1,0:T(4,128)(2,1)} %param.12), channel_id=1, source_target_pairs={{0,1},{1,2},{2,3},{3,4},{4,5},{5,6},{6,7},{7,8},{8,9},{9,10},{10,1... | collective-permute-start | bytes 442376 | tf_op jit(solution)/shard_map/ppermute | solution.py:18
  85.4 5.1 %collective-permute-start.2 = (bf16[1,3,2048]{2,1,0:T(4,128)(2,1)S(1)}, bf16[1,3,2048]{2,1,0:T(4,128)(2,1)}, u32[]{:S(2)}, u32[]{:S(2)}) collective-permute-start(bf16[1,3,2048]{2,1,0:T(4,128)(2,1)S(1)} %bitcast.169), channel_id=1, source_target_pairs={{0,1},{1,2},{2,3},{3,4},{4,5},{5,6},{6,7},{7,8},{8,9},{9,10},{10,1... | collective-permute-start | bytes 36872 | tf_op jit(solution)/shard_map/ppermute | solution.py:18
  107.0 4.9 %reshape.391 = bf16[96,1152]{1,0:T(8,128)(2,1)} reshape(bf16[8,12,96,12]{3,2,1,0:T(8,128)(2,1)S(1)} %copy.180) | data formatting | bytes 442368 | tf_op jit(solution)/shard_map/reshape | solution.py:117
  122.3 4.3 %all-to-all-start.10 = ((bf16[8,4,2,1152]{3,2,1,0:T(2,128)(2,1)}), bf16[8,4,2,1152]{3,2,1,0:T(2,128)(2,1)S(1)}, u32[]{:S(2)}, u32[]{:S(2)}) async-start(bf16[8,4,2,1152]{3,2,1,0:T(2,128)(2,1)} %reshape.343), calls=%async_computation.10 | async-start | bytes 294912 | tf_op jit(solution)/shard_map/all_to_all | solution.py:71
  127.2 6.4 %all-to-all-done.10 = bf16[8,4,2,1152]{3,2,1,0:T(2,128)(2,1)S(1)} async-done(((bf16[8,4,2,1152]{3,2,1,0:T(2,128)(2,1)}), bf16[8,4,2,1152]{3,2,1,0:T(2,128)(2,1)S(1)}, u32[]{:S(2)}, u32[]{:S(2)}) %all-to-all-start.10) | async-done | bytes 147488 | tf_op jit(solution)/shard_map/all_to_all | solution.py:71
  139.2 8.2 %all-to-all-done.6 = bf16[8,4,4,1152]{3,2,1,0:T(4,128)(2,1)S(1)} async-done(((bf16[8,4,4,1152]{3,2,1,0:T(4,128)(2,1)}), bf16[8,4,4,1152]{3,2,1,0:T(4,128)(2,1)S(1)}, u32[]{:S(2)}, u32[]{:S(2)}) %all-to-all-start.6) | async-done | bytes 294944 | tf_op jit(solution)/shard_map/all_to_all | solution.py:71
  147.4 4.1 %all-to-all-start.11 = ((bf16[8,4,2,1152]{3,2,0,1:T(2,128)(2,1)}), bf16[8,4,2,1152]{3,2,0,1:T(2,128)(2,1)S(1)}, u32[]{:S(2)}, u32[]{:S(2)}) async-start(bf16[8,4,2,1152]{3,2,0,1:T(2,128)(2,1)} %copy.197), calls=%async_computation.11 | async-start | bytes 294912 | tf_op jit(solution)/shard_map/all_to_all | solution.py:70
  160.7 141.4 %while.10 = (s32[]{:T(128)}, f32[8,12,3,256]{3,1,2,0:T(8,128)}, s32[8]{0:T(128)S(1)}, s32[8,6]{1,0:T(8,128)}, bf16[12,3,24,256]{3,0,2,1:T(8,128)(2,1)S(1)}, /*in...) while((s32[]{:T(128)}, f32[8,12,3,256]{3,1,2,0:T(8,128)}, ...), condition=%wide.region_18.19_spmd, body=%wide.region_16.18_spmd.sunk | while | flops 106955816 | bytes 24042856 | solution.py:150
  171.2 7.2 %fusion.96 = f32[8,12,3,256]{3,1,2,0:T(8,128)} fusion(f32[8,12,3,256]{3,1,2,0:T(8,128)} %get-tuple-element.168, s32[]{:T(128)S(6)} %copy.275, f32[6,256,256]{2,1,0:T(8,128)} %get-tuple-element.154, f32[6,256,256]{2,1,0:T(8,128)S(1)} %get-tuple-element.155, f32[6,3,256,256]{3,2,1,0:T(8,128)} %get-tuple-element.156, f32[3,3]{1,0:T(4,128)S(1)} %fusion.95, ...), kind=kOutput, calls=%fused_computation.17.clone.1 | convolution fusion | flops 102629376 | bytes 12742696 | tf_op jit(solution)/shard_map/while/body/eval_jaxpr/kijpq,cjkq->cip/dot_general | solution.py:148
  188.9 7.2 %fusion.96 = f32[8,12,3,256]{3,1,2,0:T(8,128)} fusion(f32[8,12,3,256]{3,1,2,0:T(8,128)} %get-tuple-element.168, s32[]{:T(128)S(6)} %copy.275, f32[6,256,256]{2,1,0:T(8,128)} %get-tuple-element.154, f32[6,256,256]{2,1,0:T(8,128)S(1)} %get-tuple-element.155, f32[6,3,256,256]{3,2,1,0:T(8,128)} %get-tuple-element.156, f32[3,3]{1,0:T(4,128)S(1)} %fusion.95, ...), kind=kOutput, calls=%fused_computation.17.clone.1 | convolution fusion | flops 102629376 | bytes 12742696 | tf_op jit(solution)/shard_map/while/body/eval_jaxpr/kijpq,cjkq->cip/dot_general | solution.py:148
  206.5 7.2 %fusion.96 = f32[8,12,3,256]{3,1,2,0:T(8,128)} fusion(f32[8,12,3,256]{3,1,2,0:T(8,128)} %get-tuple-element.168, s32[]{:T(128)S(6)} %copy.275, f32[6,256,256]{2,1,0:T(8,128)} %get-tuple-element.154, f32[6,256,256]{2,1,0:T(8,128)S(1)} %get-tuple-element.155, f32[6,3,256,256]{3,2,1,0:T(8,128)} %get-tuple-element.156, f32[3,3]{1,0:T(4,128)S(1)} %fusion.95, ...), kind=kOutput, calls=%fused_computation.17.clone.1 | convolution fusion | flops 102629376 | bytes 12742696 | tf_op jit(solution)/shard_map/while/body/eval_jaxpr/kijpq,cjkq->cip/dot_general | solution.py:148
  224.2 7.2 %fusion.96 = f32[8,12,3,256]{3,1,2,0:T(8,128)} fusion(f32[8,12,3,256]{3,1,2,0:T(8,128)} %get-tuple-element.168, s32[]{:T(128)S(6)} %copy.275, f32[6,256,256]{2,1,0:T(8,128)} %get-tuple-element.154, f32[6,256,256]{2,1,0:T(8,128)S(1)} %get-tuple-element.155, f32[6,3,256,256]{3,2,1,0:T(8,128)} %get-tuple-element.156, f32[3,3]{1,0:T(4,128)S(1)} %fusion.95, ...), kind=kOutput, calls=%fused_computation.17.clone.1 | convolution fusion | flops 102629376 | bytes 12742696 | tf_op jit(solution)/shard_map/while/body/eval_jaxpr/kijpq,cjkq->cip/dot_general | solution.py:148
  241.9 7.2 %fusion.96 = f32[8,12,3,256]{3,1,2,0:T(8,128)} fusion(f32[8,12,3,256]{3,1,2,0:T(8,128)} %get-tuple-element.168, s32[]{:T(128)S(6)} %copy.275, f32[6,256,256]{2,1,0:T(8,128)} %get-tuple-element.154, f32[6,256,256]{2,1,0:T(8,128)S(1)} %get-tuple-element.155, f32[6,3,256,256]{3,2,1,0:T(8,128)} %get-tuple-element.156, f32[3,3]{1,0:T(4,128)S(1)} %fusion.95, ...), kind=kOutput, calls=%fused_computation.17.clone.1 | convolution fusion | flops 102629376 | bytes 12742696 | tf_op jit(solution)/shard_map/while/body/eval_jaxpr/kijpq,cjkq->cip/dot_general | solution.py:148
  259.5 7.2 %fusion.96 = f32[8,12,3,256]{3,1,2,0:T(8,128)} fusion(f32[8,12,3,256]{3,1,2,0:T(8,128)} %get-tuple-element.168, s32[]{:T(128)S(6)} %copy.275, f32[6,256,256]{2,1,0:T(8,128)} %get-tuple-element.154, f32[6,256,256]{2,1,0:T(8,128)S(1)} %get-tuple-element.155, f32[6,3,256,256]{3,2,1,0:T(8,128)} %get-tuple-element.156, f32[3,3]{1,0:T(4,128)S(1)} %fusion.95, ...), kind=kOutput, calls=%fused_computation.17.clone.1 | convolution fusion | flops 102629376 | bytes 12742696 | tf_op jit(solution)/shard_map/while/body/eval_jaxpr/kijpq,cjkq->cip/dot_general | solution.py:148
  277.2 7.2 %fusion.96 = f32[8,12,3,256]{3,1,2,0:T(8,128)} fusion(f32[8,12,3,256]{3,1,2,0:T(8,128)} %get-tuple-element.168, s32[]{:T(128)S(6)} %copy.275, f32[6,256,256]{2,1,0:T(8,128)} %get-tuple-element.154, f32[6,256,256]{2,1,0:T(8,128)S(1)} %get-tuple-element.155, f32[6,3,256,256]{3,2,1,0:T(8,128)} %get-tuple-element.156, f32[3,3]{1,0:T(4,128)S(1)} %fusion.95, ...), kind=kOutput, calls=%fused_computation.17.clone.1 | convolution fusion | flops 102629376 | bytes 12742696 | tf_op jit(solution)/shard_map/while/body/eval_jaxpr/kijpq,cjkq->cip/dot_general | solution.py:148
  294.9 7.2 %fusion.96 = f32[8,12,3,256]{3,1,2,0:T(8,128)} fusion(f32[8,12,3,256]{3,1,2,0:T(8,128)} %get-tuple-element.168, s32[]{:T(128)S(6)} %copy.275, f32[6,256,256]{2,1,0:T(8,128)} %get-tuple-element.154, f32[6,256,256]{2,1,0:T(8,128)S(1)} %get-tuple-element.155, f32[6,3,256,256]{3,2,1,0:T(8,128)} %get-tuple-element.156, f32[3,3]{1,0:T(4,128)S(1)} %fusion.95, ...), kind=kOutput, calls=%fused_computation.17.clone.1 | convolution fusion | flops 102629376 | bytes 12742696 | tf_op jit(solution)/shard_map/while/body/eval_jaxpr/kijpq,cjkq->cip/dot_general | solution.py:148
  311.4 10.4 %all-to-all-done.2 = bf16[8,4,6,1152]{3,1,2,0:T(4,128)(2,1)S(1)} async-done(((bf16[8,4,6,1152]{3,1,2,0:T(4,128)(2,1)}), bf16[8,4,6,1152]{3,1,2,0:T(4,128)(2,1)S(1)}, u32[]{:S(2)}, u32[]{:S(2)}) %all-to-all-start.2) | async-done | bytes 442400 | tf_op jit(solution)/shard_map/all_to_all | solution.py:71
  322.6 4.1 %all-to-all-start.3 = ((bf16[8,4,6,1152]{3,0,2,1:T(8,128)(2,1)}), bf16[8,4,6,1152]{3,0,2,1:T(8,128)(2,1)S(1)}, u32[]{:S(2)}, u32[]{:S(2)}) async-start(bf16[8,4,6,1152]{3,0,2,1:T(8,128)(2,1)} %copy.182), calls=%async_computation.3 | async-start | bytes 884736 | tf_op jit(solution)/shard_map/all_to_all | solution.py:70
  327.2 6.4 %all-to-all-done.3 = bf16[8,4,6,1152]{3,0,2,1:T(8,128)(2,1)S(1)} async-done(((bf16[8,4,6,1152]{3,0,2,1:T(8,128)(2,1)}), bf16[8,4,6,1152]{3,0,2,1:T(8,128)(2,1)S(1)}, u32[]{:S(2)}, u32[]{:S(2)}) %all-to-all-start.3) | async-done | bytes 442400 | tf_op jit(solution)/shard_map/all_to_all | solution.py:70
  (278 shorter events, 177.7 us)
Async XLA Ops:
  3.8 13.4 %all-to-all-start.12 = ((s32[8,4,1]{1,2,0:T(1,128)}), s32[8,4,1]{1,2,0:T(1,128)S(1)}, u32[]{:S(2)}, u32[]{:S(2)}) async-start(s32[8,4,1]{1,2,0:T(1,128)} %bitcast.43), calls=%async_computation.12 | async-start | bytes 8192 | tf_op jit(solution)/shard_map/all_to_all | solution.py:78
  13.1 43.8 %slice-start.3 = ((s32[15,12]{1,0:T(8,128)}), s32[8,12]{1,0:T(8,128)S(1)}, s32[]{:S(2)}) async-start(s32[15,12]{1,0:T(8,128)} %param.20), calls=%async_computation.19 | async-start | bytes 8192 | tf_op jit(solution)/shard_map/slice | solution.py:119
  16.2 54.3 %copy-start.21 = (s32[24]{0:T(128)}, s32[24]{0:T(128)S(1)}, u32[]{:S(2)}) copy-start(s32[24]{0:T(128)S(1)} %fusion.56) | copy-start | bytes 292
  17.8 8.3 %all-to-all-start.13 = ((s32[8,4,1]{0,2,1:T(1,128)}), s32[8,4,1]{0,2,1:T(1,128)S(1)}, u32[]{:S(2)}, u32[]{:S(2)}) async-start(s32[8,4,1]{0,2,1:T(1,128)} %copy.202), calls=%async_computation.13 | async-start | bytes 4096 | tf_op jit(solution)/shard_map/all_to_all | solution.py:77
  26.1 44.4 %copy-start.18 = (s32[8,4,1]{0,2,1:T(1,128)}, s32[8,4,1]{0,2,1:T(1,128)S(1)}, u32[]{:S(2)}) copy-start(s32[8,4,1]{0,2,1:T(1,128)S(1)} %all-to-all-done.13) | copy-start | bytes 388
  26.1 10.7 %all-to-all-start.8 = ((s32[8,4,2]{1,2,0:T(2,128)}), s32[8,4,2]{1,2,0:T(2,128)S(1)}, u32[]{:S(2)}, u32[]{:S(2)}) async-start(s32[8,4,2]{1,2,0:T(2,128)} %copy.193), calls=%async_computation.8 | async-start | bytes 16384 | tf_op jit(solution)/shard_map/all_to_all | solution.py:78
  31.2 39.3 %copy-start.22 = (s32[48]{0:T(128)}, s32[48]{0:T(128)S(1)}, u32[]{:S(2)}) copy-start(s32[48]{0:T(128)S(1)} %fusion.55) | copy-start | bytes 580
  36.8 8.9 %all-to-all-start.4 = ((s32[8,4,4]{2,1,0:T(4,128)}), s32[8,4,4]{2,1,0:T(4,128)S(1)}, u32[]{:S(2)}, u32[]{:S(2)}) async-start(s32[8,4,4]{2,1,0:T(4,128)} %reshape.336), calls=%async_computation.4 | async-start | bytes 32768 | tf_op jit(solution)/shard_map/all_to_all | solution.py:78
  45.8 7.9 %all-to-all-start.9 = ((s32[8,4,2]{0,2,1:T(2,128)}), s32[8,4,2]{0,2,1:T(2,128)S(1)}, u32[]{:S(2)}, u32[]{:S(2)}) async-start(s32[8,4,2]{0,2,1:T(2,128)} %copy.194), calls=%async_computation.9 | async-start | bytes 8192 | tf_op jit(solution)/shard_map/all_to_all | solution.py:77
  53.6 7.9 %all-to-all-start.5 = ((s32[8,4,4]{0,2,1:T(4,128)}), s32[8,4,4]{0,2,1:T(4,128)S(1)}, u32[]{:S(2)}, u32[]{:S(2)}) async-start(s32[8,4,4]{0,2,1:T(4,128)} %copy.186), calls=%async_computation.5 | async-start | bytes 16384 | tf_op jit(solution)/shard_map/all_to_all | solution.py:77
  62.1 10.4 %all-to-all-start = ((s32[8,4,6]{2,1,0:T(4,128)}), s32[8,4,6]{2,1,0:T(4,128)S(1)}, u32[]{:S(2)}, u32[]{:S(2)}) async-start(s32[8,4,6]{2,1,0:T(4,128)} %reshape.327), calls=%async_computation | async-start | bytes 32768 | tf_op jit(solution)/shard_map/all_to_all | solution.py:78
  72.5 18.6 %all-to-all-start.14 = ((bf16[8,4,1,1152]{3,1,2,0:T(4,128)(2,1)}), bf16[8,4,1,1152]{3,1,2,0:T(4,128)(2,1)S(1)}, u32[]{:S(2)}, u32[]{:S(2)}) async-start(bf16[8,4,1,1152]{3,1,2,0:T(4,128)(2,1)} %bitcast.44), calls=%async_computation.14 | async-start | bytes 147456 | tf_op jit(solution)/shard_map/all_to_all | solution.py:71
  77.6 73.9 %collective-permute-start.1 = (bf16[12,3,2048]{2,1,0:T(4,128)(2,1)}, bf16[12,3,2048]{2,1,0:T(4,128)(2,1)}, u32[]{:S(2)}, u32[]{:S(2)}) collective-permute-start(bf16[12,3,2048]{2,1,0:T(4,128)(2,1)} %param.12), channel_id=1, source_target_pairs={{1,0},{2,1},{3,2},{4,3},{5,4},{6,5},{7,6},{8,7},{9,8},{10,9},{11,1... | collective-permute-start | bytes 442376 | tf_op jit(solution)/shard_map/ppermute | solution.py:21
  78.8 72.7 %collective-permute-start = (bf16[12,3,2048]{2,1,0:T(4,128)(2,1)}, bf16[12,3,2048]{2,1,0:T(4,128)(2,1)}, u32[]{:S(2)}, u32[]{:S(2)}) collective-permute-start(bf16[12,3,2048]{2,1,0:T(4,128)(2,1)} %param.12), channel_id=1, source_target_pairs={{0,1},{1,2},{2,3},{3,4},{4,5},{5,6},{6,7},{7,8},{8,9},{9,10},{10,1... | collective-permute-start | bytes 442376 | tf_op jit(solution)/shard_map/ppermute | solution.py:18
  84.1 52.9 %collective-permute-start.3 = (bf16[1,3,2048]{2,1,0:T(4,128)(2,1)S(1)}, bf16[1,3,2048]{2,1,0:T(4,128)(2,1)}, u32[]{:S(2)}, u32[]{:S(2)}) collective-permute-start(bf16[1,3,2048]{2,1,0:T(4,128)(2,1)S(1)} %bitcast.168), channel_id=1, source_target_pairs={{1,0},{2,1},{3,2},{4,3},{5,4},{6,5},{7,6},{8,7},{9,8},{10,9},{11,1... | collective-permute-start | bytes 36872 | tf_op jit(solution)/shard_map/ppermute | solution.py:21
  85.4 51.6 %collective-permute-start.2 = (bf16[1,3,2048]{2,1,0:T(4,128)(2,1)S(1)}, bf16[1,3,2048]{2,1,0:T(4,128)(2,1)}, u32[]{:S(2)}, u32[]{:S(2)}) collective-permute-start(bf16[1,3,2048]{2,1,0:T(4,128)(2,1)S(1)} %bitcast.169), channel_id=1, source_target_pairs={{0,1},{1,2},{2,3},{3,4},{4,5},{5,6},{6,7},{7,8},{8,9},{9,10},{10,1... | collective-permute-start | bytes 36872 | tf_op jit(solution)/shard_map/ppermute | solution.py:18
  91.1 7.9 %all-to-all-start.1 = ((s32[8,4,6]{2,0,1:T(8,128)}), s32[8,4,6]{2,0,1:T(8,128)S(1)}, u32[]{:S(2)}, u32[]{:S(2)}) async-start(s32[8,4,6]{2,0,1:T(8,128)} %copy.170), calls=%async_computation.1 | async-start | bytes 32768 | tf_op jit(solution)/shard_map/all_to_all | solution.py:77
  99.1 23.2 %all-to-all-start.15 = ((bf16[8,4,1,1152]{3,0,2,1:T(8,128)(2,1)}), bf16[8,4,1,1152]{3,0,2,1:T(8,128)(2,1)}, u32[]{:S(2)}, u32[]{:S(2)}) async-start(bf16[8,4,1,1152]{3,0,2,1:T(8,128)(2,1)} %copy.205), calls=%async_computation.15 | async-start | bytes 147456 | tf_op jit(solution)/shard_map/all_to_all | solution.py:70
  122.3 11.3 %all-to-all-start.10 = ((bf16[8,4,2,1152]{3,2,1,0:T(2,128)(2,1)}), bf16[8,4,2,1152]{3,2,1,0:T(2,128)(2,1)S(1)}, u32[]{:S(2)}, u32[]{:S(2)}) async-start(bf16[8,4,2,1152]{3,2,1,0:T(2,128)(2,1)} %reshape.343), calls=%async_computation.10 | async-start | bytes 294912 | tf_op jit(solution)/shard_map/all_to_all | solution.py:71
  133.6 13.8 %all-to-all-start.6 = ((bf16[8,4,4,1152]{3,2,1,0:T(4,128)(2,1)}), bf16[8,4,4,1152]{3,2,1,0:T(4,128)(2,1)S(1)}, u32[]{:S(2)}, u32[]{:S(2)}) async-start(bf16[8,4,4,1152]{3,2,1,0:T(4,128)(2,1)} %reshape.338), calls=%async_computation.6 | async-start | bytes 589824 | tf_op jit(solution)/shard_map/all_to_all | solution.py:71
  147.4 9.2 %all-to-all-start.11 = ((bf16[8,4,2,1152]{3,2,0,1:T(2,128)(2,1)}), bf16[8,4,2,1152]{3,2,0,1:T(2,128)(2,1)S(1)}, u32[]{:S(2)}, u32[]{:S(2)}) async-start(bf16[8,4,2,1152]{3,2,0,1:T(2,128)(2,1)} %copy.197), calls=%async_computation.11 | async-start | bytes 294912 | tf_op jit(solution)/shard_map/all_to_all | solution.py:70
  156.6 148.2 %all-to-all-start.7 = ((bf16[8,4,4,1152]{3,2,0,1:T(4,128)(2,1)}), bf16[8,4,4,1152]{3,2,0,1:T(4,128)(2,1)}, u32[]{:S(2)}, u32[]{:S(2)}) async-start(bf16[8,4,4,1152]{3,2,0,1:T(4,128)(2,1)} %copy.189), calls=%async_computation.7 | async-start | bytes 589824 | tf_op jit(solution)/shard_map/all_to_all | solution.py:70
  304.8 17.0 %all-to-all-start.2 = ((bf16[8,4,6,1152]{3,1,2,0:T(4,128)(2,1)}), bf16[8,4,6,1152]{3,1,2,0:T(4,128)(2,1)S(1)}, u32[]{:S(2)}, u32[]{:S(2)}) async-start(bf16[8,4,6,1152]{3,1,2,0:T(4,128)(2,1)} %copy.181), calls=%async_computation.2 | async-start | bytes 884736 | tf_op jit(solution)/shard_map/all_to_all | solution.py:71
  322.6 11.0 %all-to-all-start.3 = ((bf16[8,4,6,1152]{3,0,2,1:T(8,128)(2,1)}), bf16[8,4,6,1152]{3,0,2,1:T(8,128)(2,1)S(1)}, u32[]{:S(2)}, u32[]{:S(2)}) async-start(bf16[8,4,6,1152]{3,0,2,1:T(8,128)(2,1)} %copy.182), calls=%async_computation.3 | async-start | bytes 884736 | tf_op jit(solution)/shard_map/all_to_all | solution.py:70
  (24 other events, 268.7 us)
where the time goes:
time: 339 us; the launch traced here: 336 us
  starting transfers between devices  77.2 us (23%)
  local copies, waits for them, and re-layouts  70.6 us (21%)
  matrix products  65.1 us (19%)
  waiting for transfers between devices  56.8 us (17%)
  other arithmetic  50.9 us (15%)
  loops' own time  14.8 us (4%)
    dot_general x8, matrix products, one_leaf(): jnp.einsum('kijpq,cjkq->cip', tile, src_loads, preferred_element_type=jnp...  57.6 us
    all_to_all x4, waiting for transfers between devices, level_route(): lax.all_to_all(buffer, 'clus', split_axis=0, concat_axis=0, tiled=True)  24.9 us
    sub x8, other arithmetic, kelvin_tile(): diff = target_pts[None, :, :, None] - source_pts[:, :, None, :]  23.9 us
    all_to_all x4, starting transfers between devices, level_route(): lax.all_to_all(labels, 'clus', split_axis=0, concat_axis=0, tiled=True)  18.1 us
    all_to_all x4, starting transfers between devices, level_route(): lax.all_to_all(buffer, 'clus', split_axis=0, concat_axis=0, tiled=True)  16.4 us
    all_to_all x4, starting transfers between devices, level_route(): lax.all_to_all(lax.all_to_all(buffer, 'clus', split_axis=0, concat_axis=0...  16.2 us
    another operation x1, loops' own time, body(): near = lax.map(one_leaf, jnp.arange(per_dev, dtype=jnp.int32))  14.8 us
    all_to_all x4, waiting for transfers between devices, level_route(): lax.all_to_all(lax.all_to_all(labels, 'clus', split_axis=0, concat_axis=0...  14.7 us
  transfers between devices with their start and end apart: 20, of which 11 were waited for; matrix products, arithmetic and copies ran while one was open for 53% of the time, Pallas kernels for 0%

commit v1 on v0

v1 whole, which is shorter than its diff:
```python
import functools
import math

import jax
import jax.numpy as jnp
from jax import lax
from jax.experimental import pallas as pl
from jax.experimental.pallas import tpu as pltpu
from jax.sharding import PartitionSpec as P

CORE_SQ = 0.0625
KELVIN = 1.0 / (16.0 * math.pi * 0.7)
SHEAR = 1.8
F32 = jnp.float32
BF16 = jnp.bfloat16
NT = (((1,), (1,)), ((), ()))
CH = 32


def dot_nt(a, b):
    return lax.dot_general(a, b, NT, preferred_element_type=F32)


def dot(a, b):
    return jnp.dot(a, b, preferred_element_type=F32)


def kernel(dims, pack, basis, up_leaf, up_mid, up_top, coup, dest, target, near_src, out,
           win, bas_v, ul_v, um_v, ut_v, coup_v, coef, labels, tab_v, tab, send, got,
           lhs, ycol, tiles, near, inc, w, in_sem, halo_send, halo_recv, a2a_send, a2a_recv):
    ndev, nsub, cap, nl, fan, rank, leaf = dims
    rows = cap * 16
    per_row = 2 * nl - 1
    nb = per_row * fan
    nbp = (nb + 15) // 16 * 16
    lin = lax.axis_index("clus") * nsub + lax.axis_index("sub")

    def place(index):
        return {"clus": index // nsub, "sub": lax.rem(index, nsub)}

    barrier = pltpu.get_barrier_semaphore()

    def greet(step, carry):
        other = lax.rem(lin + step, ndev)
        pl.semaphore_signal(barrier, inc=1, device_id=place(other), device_id_type=pl.DeviceIdType.MESH)
        return carry

    loads_in = [
        pltpu.make_async_copy(pack, win.at[1], in_sem.at[0]),
        pltpu.make_async_copy(basis, bas_v, in_sem.at[1]),
        pltpu.make_async_copy(up_leaf, ul_v, in_sem.at[2]),
        pltpu.make_async_copy(up_mid, um_v, in_sem.at[3]),
        pltpu.make_async_copy(up_top, ut_v, in_sem.at[4]),
        pltpu.make_async_copy(coup, coup_v, in_sem.at[5]),
    ]
    for copy in loads_in:
        copy.start()
    lax.fori_loop(1, ndev, greet, 0)

    row_i = lax.broadcasted_iota(jnp.int32, (per_row, fan), 0)
    off = jnp.where(row_i < nl, 0, jnp.where(row_i < nl + nl // 2, nl, jnp.where(row_i < per_row - 1, nl + nl // 2, per_row - 1)))
    goal = ((target[...] + off) * 16).astype(F32)
    dst = dest[...].astype(F32)
    b_row = lax.broadcasted_iota(jnp.int32, (nbp, per_row), 0) // fan
    pick_r = (b_row == lax.broadcasted_iota(jnp.int32, (nbp, per_row), 1)).astype(F32)
    b_fan = lax.rem(lax.broadcasted_iota(jnp.int32, (nbp, fan), 0), fan)
    pick_k = b_fan == lax.broadcasted_iota(jnp.int32, (nbp, fan), 1)
    valid = lax.broadcasted_iota(jnp.int32, (nbp, 1), 0) < nb

    def column(values):
        spread = dot(pick_r.astype(BF16), values.astype(BF16))
        return jnp.sum(jnp.where(pick_k, spread, 0.0), axis=1, keepdims=True)

    dest_c = jnp.where(valid, column(dst), -1.0)
    goal_c = column(goal)
    sub_b = lax.broadcasted_iota(jnp.int32, (nbp, nbp), 0)
    lane_b = lax.broadcasted_iota(jnp.int32, (nbp, nbp), 1)
    dest_r = jnp.sum(jnp.where(sub_b == lane_b, dest_c, 0.0), axis=0, keepdims=True)
    rank_c = jnp.sum(jnp.where((dest_c == dest_r) & (lane_b < sub_b), 1.0, 0.0), axis=1, keepdims=True)
    lane = lax.broadcasted_iota(jnp.int32, (nbp, 128), 1)
    number = lax.broadcasted_iota(jnp.int32, (nbp, 128), 0).astype(F32)
    slot_of = (lane // 16).astype(F32)
    hits = rank_c == slot_of
    tag_w = jnp.where(hits & (lane < rows), goal_c + 1.0, 0.0).astype(BF16)
    num_w = jnp.where(rank_c == lane.astype(F32), number, 0.0).astype(BF16)
    who = lax.broadcasted_iota(jnp.int32, (ndev, nbp), 0).astype(F32)
    mine = (who == dest_r).astype(F32).astype(BF16)
    tags = dot(mine, tag_w)
    lane_d = lax.broadcasted_iota(jnp.int32, (ndev, 128), 1)
    comp = lax.rem(lane_d, 16)
    labels[...] = jnp.where((tags > 0.5) & (comp < 12), tags - 1.0 + comp.astype(F32), 255.0)
    tab_v[...] = dot(mine, num_w).astype(jnp.int32)
    to_smem = pltpu.make_async_copy(tab_v, tab, in_sem.at[6])
    to_smem.start()

    loads_in[0].wait()
    loads_in[1].wait()
    for t in range(nl):
        total = jnp.zeros((16, rank), F32)
        for i in range(3):
            total += dot_nt(win[1, i, :, t * leaf:(t + 1) * leaf], bas_v[t, i])
        coef[t] = total.astype(BF16)
    for copy in loads_in[2:5]:
        copy.wait()
    lower, upper = 0, nl
    for mats, count in ((ul_v, nl), (um_v, nl // 2), (ut_v, nl // 4)):
        for k in range(count // 2):
            total = dot_nt(coef[lower + 2 * k], mats[2 * k]) + dot_nt(coef[lower + 2 * k + 1], mats[2 * k + 1])
            coef[upper + k] = total.astype(BF16)
        lower, upper = upper, upper + count // 2

    pl.semaphore_wait(barrier, ndev - 1)
    right = lax.rem(lin + 1, ndev)
    left = lax.rem(lin + ndev - 1, ndev)
    to_right = pltpu.make_async_remote_copy(
        src_ref=win.at[1], dst_ref=win.at[0], send_sem=halo_send.at[0], recv_sem=halo_recv.at[0],
        device_id=place(right), device_id_type=pl.DeviceIdType.MESH)
    to_left = pltpu.make_async_remote_copy(
        src_ref=win.at[1], dst_ref=win.at[2], send_sem=halo_send.at[1], recv_sem=halo_recv.at[1],
        device_id=place(left), device_id_type=pl.DeviceIdType.MESH)
    to_right.start()
    to_left.start()

    to_smem.wait()
    loads_in[5].wait()
    mark = lax.broadcasted_iota(jnp.int32, (16, rank), 0) == 12

    def make_block(other, store):
        for s in range(cap):
            b = jnp.clip(tab[other, s], 0, nb - 1)
            prod = dot_nt(coef[lax.div(b, fan)], coup_v[b])
            if s == 0:
                prod = jnp.where(mark, labels[pl.ds(other, 1), :rank], prod)
            store(s, prod.astype(BF16))

    def far_copy(step):
        other = lax.rem(lin + step, ndev)
        return pltpu.make_async_remote_copy(
            src_ref=send.at[step], dst_ref=got.at[step], send_sem=a2a_send.at[step], recv_sem=a2a_recv.at[step],
            device_id=place(other), device_id_type=pl.DeviceIdType.MESH)

    def couple(step, carry):
        def store(s, value):
            send[step, s * 16:(s + 1) * 16] = value
        make_block(lax.rem(lin + step, ndev), store)
        far_copy(step).start()
        return carry

    lax.fori_loop(1, ndev, couple, 0)

    def store_own(s, value):
        got[0, s * 16:(s + 1) * 16] = value
    make_block(lin, store_own)

    to_right.wait()
    to_left.wait()
    for part in range(3):
        def prepare(t, carry):
            cols = pl.ds(pl.multiple_of(t * leaf, leaf), leaf)
            cen = win[part, 3, :, cols].astype(F32)
            ycol[part * nl + t] = cen.T
            for j in range(3):
                f = win[part, j, :, cols]
                lhs[part * nl + t, j, 0:16] = f
                f32 = f.astype(F32)
                for i in range(3):
                    prod = f32 * cen[i:i + 1]
                    high = prod.astype(BF16)
                    lhs[part * nl + t, j, 16 + 16 * i:32 + 16 * i] = high
                    lhs[part * nl + t, j, 64 + 16 * i:80 + 16 * i] = (prod - high.astype(F32)).astype(BF16)
            return carry
        lax.fori_loop(0, nl, prepare, 0)

    base = lin * nl - nl
    n_near = near_src.shape[1]

    def near_leaf(t, carry):
        cols = pl.ds(pl.multiple_of(t * leaf, leaf), leaf)
        own = win[1, 3, :, cols].astype(F32)
        x = [own[i:i + 1] for i in range(3)]
        acc = jnp.zeros((112, leaf), F32)
        acc_r = [jnp.zeros((16, leaf), F32) for _ in range(3)]
        for k in range(n_near):
            s = jnp.clip(near_src[t, k] - base, 0, 3 * nl - 1)
            for c in range(leaf // CH):
                y = ycol[s, c * CH:(c + 1) * CH, :]
                v = [x[i] - y[:, i:i + 1] for i in range(3)]
                r = lax.rsqrt(v[0] * v[0] + v[1] * v[1] + v[2] * v[2] + CORE_SQ)
                kr = r * KELVIN
                rr = r * r
                tiles[k % 2, 3, c * CH:(c + 1) * CH] = (kr * SHEAR).astype(BF16)
                for j in range(3):
                    tiles[k % 2, j, c * CH:(c + 1) * CH] = ((v[j] * rr) * kr).astype(BF16)
            for j in range(3):
                acc += dot(lhs[s, j], tiles[k % 2, j])
                acc_r[j] += dot(lhs[s, j, 0:16], tiles[k % 2, 3])
        for i in range(3):
            part = acc[0:16] * x[i] - (acc[16 + 16 * i:32 + 16 * i] + acc[64 + 16 * i:80 + 16 * i])
            near[i, :, cols] = acc_r[i] + part
        return carry

    lax.fori_loop(0, nl, near_leaf, 0)

    inc[...] = jnp.zeros_like(inc)
    q_row = lax.broadcasted_iota(jnp.int32, (per_row * 16, rows), 0).astype(F32)

    def add_block(step):
        tag = got[step, 0:16, :rows].astype(F32)[12:13]
        pick = jnp.where(q_row == tag, 1.0, 0.0).astype(BF16)
        inc[...] += dot(pick, got[step])

    add_block(0)

    def collect(step, carry):
        far_copy(step).wait()
        add_block(step)
        return carry

    lax.fori_loop(1, ndev, collect, 0)

    w[per_row - 1] = inc[(per_row - 1) * 16:per_row * 16].astype(BF16)
    upper = per_row - 1
    for mats, count in ((ut_v, nl // 4), (um_v, nl // 2), (ul_v, nl)):
        lower = upper - count
        for k in range(count):
            q = lower + k
            w[q] = (inc[q * 16:(q + 1) * 16] + dot(w[upper + k // 2], mats[k])).astype(BF16)
        upper = lower
    for t in range(nl):
        for i in range(3):
            out[i, :, t * leaf:(t + 1) * leaf] = near[i, :, t * leaf:(t + 1) * leaf] + dot(w[t], bas_v[t, i])


def body(loads, centers, basis, up_leaf, up_mid, up_top, couplings, far_dest, far_target, near_src):
    cases = loads.shape[0]
    nl, rank, _, leaf = basis.shape
    nsub = lax.axis_size("sub")
    ndev = lax.axis_size("clus") * nsub
    per_row, fan = far_dest.shape
    cap = max(2, (per_row * fan + ndev - 1) // ndev)
    rows = cap * 16
    width = nl * leaf
    pack = jnp.concatenate([
        jnp.pad(jnp.transpose(loads, (1, 0, 2)), ((0, 0), (0, 16 - cases), (0, 0))),
        jnp.pad(centers[None], ((0, 0), (0, 13), (0, 0))),
    ], axis=0)
    dims = (ndev, nsub, cap, nl, fan, rank, leaf)
    hbm = pl.BlockSpec(memory_space=pl.ANY)
    vmem = pl.BlockSpec(memory_space=pltpu.VMEM)
    smem = pl.BlockSpec(memory_space=pltpu.SMEM)
    out = pl.pallas_call(
        functools.partial(kernel, dims),
        out_shape=jax.ShapeDtypeStruct((3, 16, width), F32),
        in_specs=[hbm] * 6 + [vmem, vmem, smem],
        out_specs=vmem,
        scratch_shapes=[
            pltpu.VMEM((3, 4, 16, width), BF16),
            pltpu.VMEM((nl, 3, rank, leaf), BF16),
            pltpu.VMEM((nl, rank, rank), BF16),
            pltpu.VMEM((nl // 2, rank, rank), BF16),
            pltpu.VMEM((nl // 4, rank, rank), BF16),
            pltpu.VMEM((per_row * fan, rank, rank), BF16),
            pltpu.VMEM((per_row, 16, rank), BF16),
            pltpu.VMEM((ndev, 128), F32),
            pltpu.VMEM((ndev, 128), jnp.int32),
            pltpu.SMEM((ndev, 128), jnp.int32),
            pltpu.VMEM((ndev, rows, rank), BF16),
            pltpu.VMEM((ndev, rows, rank), BF16),
            pltpu.VMEM((3 * nl, 3, 112, leaf), BF16),
            pltpu.VMEM((3 * nl, leaf, 16), F32),
            pltpu.VMEM((2, 4, leaf, leaf), BF16),
            pltpu.VMEM((3, 16, width), F32),
            pltpu.VMEM((per_row * 16, rank), F32),
            pltpu.VMEM((per_row, 16, rank), BF16),
            pltpu.SemaphoreType.DMA((7,)),
            pltpu.SemaphoreType.DMA((2,)),
            pltpu.SemaphoreType.DMA((2,)),
            pltpu.SemaphoreType.DMA((ndev,)),
            pltpu.SemaphoreType.DMA((ndev,)),
        ],
        compiler_params=pltpu.CompilerParams(
            collective_id=0, has_side_effects=True, vmem_limit_bytes=50 * 1024 * 1024
        ),
    )(pack, jnp.transpose(basis, (0, 2, 1, 3)), up_leaf, up_mid, up_top,
      couplings.reshape(per_row * fan, rank, rank), far_dest, far_target, near_src)
    return jnp.transpose(out[:, :cases], (1, 0, 2))


def solution(mesh):
    every = ("groups", "clus", "sub")
    return jax.shard_map(
        body,
        mesh=mesh,
        in_specs=(
            P(None, None, every),
            P(None, every),
            P(every, None, None, None),
            P(every, None, None),
            P(every, None, None),
            P(every, None, None),
            P(every, None, None, None),
            P(every, None),
            P(every, None),
            P(every, None),
        ),
        out_specs=P(None, None, every),
        check_vma=False,
    )
```

time: 339 us -> 60.8 us (0.18)
  starting transfers between devices: 77.2 us -> 0 us
  matrix products: 65.1 us -> 0 us
  local copies, waits for them, and re-layouts: 70.6 us -> 7.98 us
  waiting for transfers between devices: 56.8 us -> 0 us
  Pallas kernels: 0 us -> 51.6 us
  other arithmetic: 50.9 us -> 0.75 us
  loops' own time: 14.8 us -> 0 us
    dot_general x20 -> x0, matrix products: 65.1 us -> none  [the longest x8 57.6 us: one_leaf(): jnp.einsum('kijpq,cjkq->cip', tile, src_loads, preferred_element_type=jnp...]
    all_to_all x16 -> x0, starting transfers between devices: 64.2 us -> none  [the longest x4 18.1 us: level_route(): lax.all_to_all(labels, 'clus', split_axis=0, concat_axis=0, tiled=True)]
    all_to_all x16 -> x0, waiting for transfers between devices: 56.8 us -> none  [the longest x4 24.9 us: level_route(): lax.all_to_all(buffer, 'clus', split_axis=0, concat_axis=0, tiled=True)]
    pallas_call x0 -> x1, Pallas kernels: none -> 51.6 us  [body(): pl.pallas_call(functools.partial(kernel, dims), out_shape=jax.ShapeDtypeS...]
    sub x9 -> x0, other arithmetic: 24.5 us -> none  [the longest x8 23.9 us: kelvin_tile(): diff = target_pts[None, :, :, None] - source_pts[:, :, None, :]]
    reshape x25 -> x0, local copies, waits for them, and re-layouts: 18.5 us -> none  [the longest x4 8.42 us: body(): contrib[lower:upper].reshape(-1, width)]
    gather x16 -> x0, local copies, waits for them, and re-layouts: 16.2 us -> none  [the longest x8 11.7 us: one_leaf(): src_pts = jnp.transpose(win_pts[:, srcs], (1, 0, 2))]
    another operation x1 -> x0, loops' own time: 14.8 us -> none  [body(): near = lax.map(one_leaf, jnp.arange(per_dev, dtype=jnp.int32))]
  transfers between devices with their start and end apart: 20 -> 0, of which waited for: 11 -> 0; matrix products, arithmetic and copies ran while one was open for 53% -> 0% of each run, Pallas kernels for 0% -> 0%
where the time goes in v1:
time: 60.8 us; the launch traced here: 60.3 us
  Pallas kernels  51.6 us (85%)
  local copies, waits for them, and re-layouts  7.98 us (13%)
  other arithmetic  0.75 us (1%)
    pallas_call x1, Pallas kernels, body(): pl.pallas_call(functools.partial(kernel, dims), out_shape=jax.ShapeDtypeS...  51.6 us
    unnamed x15, local copies, waits for them, and re-layouts  7 us

profile of v1, /device:TPU:0, one launch (start us, length us, event | category | flops | bytes accessed | tf_op | source)
XLA Modules:
  0.0 60.3 jit_solution(5785221152781473432)
XLA Ops:
  0.0 1.0 %copy.14 = bf16[12,3,2048]{2,0,1:T(8,128)(2,1)S(1)} copy(bf16[12,3,2048]{2,1,0:T(4,128)(2,1)} %param.10) | data formatting | bytes 294912 | tf_op args[0]
  1.0 0.7 %fusion.2.pack = bf16[4,16,2048]{2,1,0:T(8,128)(2,1)S(1)} fusion(bf16[1,3,2048]{2,1,0:T(4,128)(2,1)} %bitcast.11, bf16[3,12,2048]{2,1,0:T(8,128)(2,1)S(1)} %bitcast.10), kind=kLoop, calls=%fused_computation.5 | loop fusion | flops 1048576 | bytes 421888 | tf_op jit(solution)/shard_map/concatenate | solution.py:243
  1.8 0.0 copy-start
  1.8 1.3 %copy-done = bf16[8,96,3,256]{3,1,2,0:T(8,128)(2,1)S(1)} copy-done((bf16[8,96,3,256]{3,1,2,0:T(8,128)(2,1)S(1)}, bf16[8,96,3,256]{3,1,2,0:T(8,128)(2,1)}, u32[]{:S(2)}) %copy-start) | copy-done | bytes 1179672
  3.1 0.0 copy-start.1
  3.1 0.9 %copy-done.1 = bf16[8,96,96]{2,1,0:T(8,128)(2,1)S(1)} copy-done((bf16[8,96,96]{2,1,0:T(8,128)(2,1)S(1)}, bf16[8,96,96]{2,1,0:T(8,128)(2,1)}, u32[]{:S(2)}) %copy-start.1) | copy-done | bytes 147480
  4.0 0.0 copy-start.2
  4.0 0.9 %copy-done.2 = bf16[4,96,96]{2,1,0:T(8,128)(2,1)S(1)} copy-done((bf16[4,96,96]{2,1,0:T(8,128)(2,1)S(1)}, bf16[4,96,96]{2,1,0:T(8,128)(2,1)}, u32[]{:S(2)}) %copy-start.2) | copy-done | bytes 73752
  4.9 0.0 copy-start.3
  4.9 0.8 %copy-done.3 = bf16[2,96,96]{2,1,0:T(8,128)(2,1)S(1)} copy-done((bf16[2,96,96]{2,1,0:T(8,128)(2,1)S(1)}, bf16[2,96,96]{2,1,0:T(8,128)(2,1)}, u32[]{:S(2)}) %copy-start.3) | copy-done | bytes 36888
  5.7 0.0 copy-start.4
  5.7 0.7 %copy-done.4 = s32[15,12]{1,0:T(8,128)S(1)} copy-done((s32[15,12]{1,0:T(8,128)S(1)}, s32[15,12]{1,0:T(8,128)}, u32[]{:S(2)}) %copy-start.4) | copy-done | bytes 744
  6.4 0.0 copy-start.5
  6.4 0.7 %copy-done.5 = s32[15,12]{1,0:T(8,128)S(1)} copy-done((s32[15,12]{1,0:T(8,128)S(1)}, s32[15,12]{1,0:T(8,128)}, u32[]{:S(2)}) %copy-start.5) | copy-done | bytes 744
  7.1 0.0 copy-start.6
  7.1 0.7 %copy-done.6 = s32[8,6]{1,0:T(8,128)S(1)} copy-done((s32[8,6]{1,0:T(8,128)S(1)}, s32[8,6]{1,0:T(8,128)}, u32[]{:S(2)}) %copy-start.6) | copy-done | bytes 216
  7.8 51.6 %shard_map.100 = f32[3,16,2048]{2,1,0:T(8,128)S(1)} custom-call(bf16[4,16,2048]{2,1,0:T(8,128)(2,1)S(1)} %fusion.2.pack, bf16[8,3,96,256]{3,2,1,0:T(8,128)(2,1)S(1)} %bitcast.8, bf16[8,96,96]{2,1,0:T(8,128)(2,1)S(1)} %copy-done.1, bf16[4,96,96]{2,1,0:T(8,128)(2,1)S(1)} %copy-done.2, bf16[2,96,96]{2,1,0:T(8,128)(2,1)S(1)} %copy-done.3, ...), custom_call_target="tpu_custom_call" | custom-call | tf_op jit(solution)/shard_map/pallas_call | solution.py:251
  59.4 0.9 %copy.12 = f32[12,3,2048]{2,1,0:T(4,128)} copy(f32[12,3,2048]{2,0,1:T(8,128)S(1)} %slice_bitcast_fusion) | data formatting | bytes 589824 | tf_op jit(solution)/shard_map/transpose | solution.py:286
  (1 shorter events, 0.0 us)
Async XLA Ops:
  1.8 1.3 %copy-start = (bf16[8,96,3,256]{3,1,2,0:T(8,128)(2,1)S(1)}, bf16[8,96,3,256]{3,1,2,0:T(8,128)(2,1)}, u32[]{:S(2)}) copy-start(bf16[8,96,3,256]{3,1,2,0:T(8,128)(2,1)} %param.12) | copy-start | bytes 3538948
  3.1 0.9 %copy-start.1 = (bf16[8,96,96]{2,1,0:T(8,128)(2,1)S(1)}, bf16[8,96,96]{2,1,0:T(8,128)(2,1)}, u32[]{:S(2)}) copy-start(bf16[8,96,96]{2,1,0:T(8,128)(2,1)} %up_leaf.1) | copy-start | bytes 442372
  4.0 0.9 %copy-start.2 = (bf16[4,96,96]{2,1,0:T(8,128)(2,1)S(1)}, bf16[4,96,96]{2,1,0:T(8,128)(2,1)}, u32[]{:S(2)}) copy-start(bf16[4,96,96]{2,1,0:T(8,128)(2,1)} %up_mid.1) | copy-start | bytes 221188
  4.9 0.8 %copy-start.3 = (bf16[2,96,96]{2,1,0:T(8,128)(2,1)S(1)}, bf16[2,96,96]{2,1,0:T(8,128)(2,1)}, u32[]{:S(2)}) copy-start(bf16[2,96,96]{2,1,0:T(8,128)(2,1)} %up_top.1) | copy-start | bytes 110596
  5.7 0.7 %copy-start.4 = (s32[15,12]{1,0:T(8,128)S(1)}, s32[15,12]{1,0:T(8,128)}, u32[]{:S(2)}) copy-start(s32[15,12]{1,0:T(8,128)} %dest.1) | copy-start | bytes 2164
  6.4 0.7 %copy-start.5 = (s32[15,12]{1,0:T(8,128)S(1)}, s32[15,12]{1,0:T(8,128)}, u32[]{:S(2)}) copy-start(s32[15,12]{1,0:T(8,128)} %target.1) | copy-start | bytes 2164
  7.1 0.7 %copy-start.6 = (s32[8,6]{1,0:T(8,128)S(1)}, s32[8,6]{1,0:T(8,128)}, u32[]{:S(2)}) copy-start(s32[8,6]{1,0:T(8,128)} %near_src.1) | copy-start | bytes 580

commit v2 on v1

v2 whole, which is shorter than its diff:
```python
import functools
import math

import jax
import jax.numpy as jnp
from jax import lax
from jax.experimental import pallas as pl
from jax.experimental.pallas import tpu as pltpu
from jax.sharding import PartitionSpec as P

CORE_SQ = 0.0625
KELVIN = 1.0 / (16.0 * math.pi * 0.7)
SHEAR = 1.8
F32 = jnp.float32
BF16 = jnp.bfloat16
NT = (((1,), (1,)), ((), ()))
CH = 32


def dot_nt(a, b):
    return lax.dot_general(a, b, NT, preferred_element_type=F32)


def dot(a, b):
    return jnp.dot(a, b, preferred_element_type=F32)


def kernel(dims, pack, basis, up_leaf, up_mid, up_top, coup, dest_h, target_h, near_h, out,
           dest, target, near_src, win, bas_v, ul_v, um_v, ut_v, coup_v, coef, labels, tab_v, tab, send, got,
           lhs, lhs_r, ycol, tiles, near, inc, w, in_sem, halo_send, halo_recv, a2a_send, a2a_recv):
    ndev, nsub, cap, nl, fan, rank, leaf = dims
    used = cap * 12
    rows = (used + 16) // 16 * 16
    per_row = 2 * nl - 1
    nb = per_row * fan
    nbp = (nb + 15) // 16 * 16
    lin = lax.axis_index("clus") * nsub + lax.axis_index("sub")

    def place(index):
        return {"clus": index // nsub, "sub": lax.rem(index, nsub)}

    barrier = pltpu.get_barrier_semaphore()

    def greet(step, carry):
        other = lax.rem(lin + step, ndev)
        pl.semaphore_signal(barrier, inc=1, device_id=place(other), device_id_type=pl.DeviceIdType.MESH)
        return carry

    loads_in = [
        pltpu.make_async_copy(pack, win.at[1], in_sem.at[0]),
        pltpu.make_async_copy(basis, bas_v, in_sem.at[1]),
        pltpu.make_async_copy(up_leaf, ul_v, in_sem.at[2]),
        pltpu.make_async_copy(up_mid, um_v, in_sem.at[3]),
        pltpu.make_async_copy(up_top, ut_v, in_sem.at[4]),
        pltpu.make_async_copy(coup, coup_v, in_sem.at[5]),
        pltpu.make_async_copy(dest_h, dest, in_sem.at[7]),
        pltpu.make_async_copy(target_h, target, in_sem.at[8]),
        pltpu.make_async_copy(near_h, near_src, in_sem.at[9]),
    ]
    lax.fori_loop(1, ndev, greet, 0)
    for index in (0, 6, 7, 1, 2, 3, 4, 8, 5):
        loads_in[index].start()

    loads_in[0].wait()
    pl.semaphore_wait(barrier, ndev - 1)
    right = lax.rem(lin + 1, ndev)
    left = lax.rem(lin + ndev - 1, ndev)
    to_right = pltpu.make_async_remote_copy(
        src_ref=win.at[1], dst_ref=win.at[0], send_sem=halo_send.at[0], recv_sem=halo_recv.at[0],
        device_id=place(right), device_id_type=pl.DeviceIdType.MESH)
    to_left = pltpu.make_async_remote_copy(
        src_ref=win.at[1], dst_ref=win.at[2], send_sem=halo_send.at[1], recv_sem=halo_recv.at[1],
        device_id=place(left), device_id_type=pl.DeviceIdType.MESH)
    to_right.start()
    to_left.start()

    loads_in[6].wait()
    loads_in[7].wait()
    row_i = lax.broadcasted_iota(jnp.int32, (per_row, fan), 0)
    off = jnp.where(row_i < nl, 0, jnp.where(row_i < nl + nl // 2, nl, jnp.where(row_i < per_row - 1, nl + nl // 2, per_row - 1)))
    goal = ((target[...] + off) * 16).astype(F32)
    dst = dest[...].astype(F32)
    b_row = lax.broadcasted_iota(jnp.int32, (nbp, per_row), 0) // fan
    pick_r = (b_row == lax.broadcasted_iota(jnp.int32, (nbp, per_row), 1)).astype(F32)
    b_fan = lax.rem(lax.broadcasted_iota(jnp.int32, (nbp, fan), 0), fan)
    pick_k = b_fan == lax.broadcasted_iota(jnp.int32, (nbp, fan), 1)
    valid = lax.broadcasted_iota(jnp.int32, (nbp, 1), 0) < nb

    def column(values):
        spread = dot(pick_r.astype(BF16), values.astype(BF16))
        return jnp.sum(jnp.where(pick_k, spread, 0.0), axis=1, keepdims=True)

    dest_c = jnp.where(valid, column(dst), -1.0)
    goal_c = column(goal)
    sub_b = lax.broadcasted_iota(jnp.int32, (nbp, nbp), 0)
    lane_b = lax.broadcasted_iota(jnp.int32, (nbp, nbp), 1)
    dest_r = jnp.sum(jnp.where(sub_b == lane_b, dest_c, 0.0), axis=0, keepdims=True)
    rank_c = jnp.sum(jnp.where((dest_c == dest_r) & (lane_b < sub_b), 1.0, 0.0), axis=1, keepdims=True)
    lane = lax.broadcasted_iota(jnp.int32, (nbp, 128), 1)
    number = lax.broadcasted_iota(jnp.int32, (nbp, 128), 0).astype(F32)
    slot_of = (lane // 12).astype(F32)
    hits = rank_c == slot_of
    tag_w = jnp.where(hits & (lane < used), goal_c + 1.0, 0.0).astype(BF16)
    num_w = jnp.where(rank_c == lane.astype(F32), number, 0.0).astype(BF16)
    who = lax.broadcasted_iota(jnp.int32, (ndev, nbp), 0).astype(F32)
    mine = (who == dest_r).astype(F32).astype(BF16)
    tags = dot(mine, tag_w)
    lane_d = lax.broadcasted_iota(jnp.int32, (ndev, 128), 1)
    comp = lax.rem(lane_d, 12)
    labels[...] = jnp.where(tags > 0.5, tags - 1.0 + comp.astype(F32), 255.0)
    tab_v[...] = dot(mine, num_w).astype(jnp.int32)
    to_smem = pltpu.make_async_copy(tab_v, tab, in_sem.at[6])
    to_smem.start()

    def cut(part, start, i):
        block = win[part, :, pl.ds(start, leaf)].astype(F32)
        return block[12 * i:12 * i + 16].astype(BF16)

    loads_in[1].wait()
    for t in range(nl):
        total = jnp.zeros((16, rank), F32)
        for i in range(3):
            total += dot_nt(cut(1, t * leaf, i), bas_v[t, i])
        coef[t] = total.astype(BF16)
    for copy in loads_in[2:5]:
        copy.wait()
    lower, upper = 0, nl
    for mats, count in ((ul_v, nl), (um_v, nl // 2), (ut_v, nl // 4)):
        for k in range(count // 2):
            total = dot_nt(coef[lower + 2 * k], mats[2 * k]) + dot_nt(coef[lower + 2 * k + 1], mats[2 * k + 1])
            coef[upper + k] = total.astype(BF16)
        lower, upper = upper, upper + count // 2

    to_smem.wait()
    loads_in[5].wait()
    def make_block(other):
        prods = []
        for s in range(cap):
            b = jnp.clip(tab[other, s], 0, nb - 1)
            prods.append(dot_nt(coef[lax.div(b, fan)], coup_v[b])[:12])
        prods.append(labels[pl.ds(other, 1), :rank])
        prods.append(jnp.zeros((rows - used - 1, rank), F32))
        return jnp.concatenate(prods, axis=0).astype(BF16)

    def far_copy(step):
        other = lax.rem(lin + step, ndev)
        return pltpu.make_async_remote_copy(
            src_ref=send.at[step], dst_ref=got.at[step], send_sem=a2a_send.at[step], recv_sem=a2a_recv.at[step],
            device_id=place(other), device_id_type=pl.DeviceIdType.MESH)

    def couple(group, carry):
        blocks = [make_block(lax.rem(lin + group * 4 + u, ndev)) for u in range(4)]
        for u in range(4):
            send[group * 4 + u] = blocks[u]
        for u in range(4):
            far_copy(group * 4 + u).start()
        return carry

    blocks = [make_block(lax.rem(lin + u, ndev)) for u in range(4)]
    got[0] = blocks[0]
    for u in range(1, 4):
        send[u] = blocks[u]
    for u in range(1, 4):
        far_copy(u).start()
    lax.fori_loop(1, ndev // 4, couple, 0)

    for part in (1, 0, 2):
        if part == 0:
            to_right.wait()
            to_left.wait()

        def prepare(t, carry):
            block = win[part, :, pl.ds(pl.multiple_of(t * leaf, leaf), leaf)].astype(F32)
            ycol[part * nl + t] = block[32:48].T
            for j in range(3):
                f = block[12 * j:12 * j + 16]
                lhs[part * nl + t, j, 0:16] = f.astype(BF16)
                lhs_r[part * nl + t, 16 * j:16 * j + 16] = f.astype(BF16)
                for i in range(3):
                    prod = f * block[36 + i:37 + i]
                    high = prod.astype(BF16)
                    lhs[part * nl + t, j, 16 + 16 * i:32 + 16 * i] = high
                    lhs[part * nl + t, j, 64 + 16 * i:80 + 16 * i] = (prod - high.astype(F32)).astype(BF16)
            return carry
        lax.fori_loop(0, nl, prepare, 0)

    loads_in[8].wait()
    base = lin * nl - nl
    n_near = near_src.shape[1]

    def near_leaf(t, carry):
        cols = pl.ds(pl.multiple_of(t * leaf, leaf), leaf)
        own = win[1, 32:48, cols].astype(F32)
        x = [own[4 + i:5 + i] for i in range(3)]
        acc = jnp.zeros((112, leaf), F32)
        acc_r = jnp.zeros((48, leaf), F32)
        srcs = [jnp.clip(near_src[t, k] - base, 0, 3 * nl - 1) for k in range(n_near)]
        chunks = leaf // CH
        for k in range(n_near + 1):
            for c in range(chunks):
                if k < n_near:
                    y = ycol[srcs[k], c * CH:(c + 1) * CH, :]
                    v = [x[i] - y[:, 4 + i:5 + i] for i in range(3)]
                    r = lax.rsqrt(v[0] * v[0] + v[1] * v[1] + v[2] * v[2] + CORE_SQ)
                    rr = r * r
                    tiles[k % 2, 3, c * CH:(c + 1) * CH] = r.astype(BF16)
                    for j in range(3):
                        tiles[k % 2, j, c * CH:(c + 1) * CH] = ((v[j] * rr) * r).astype(BF16)
                if k > 0 and c % (chunks // 4) == 0:
                    j = c // (chunks // 4)
                    if j < 3:
                        acc += dot(lhs[srcs[k - 1], j], tiles[(k - 1) % 2, j])
                    else:
                        acc_r += dot(lhs_r[srcs[k - 1]], tiles[(k - 1) % 2, 3])
        for i in range(3):
            part = acc[0:16] * x[i] - (acc[16 + 16 * i:32 + 16 * i] + acc[64 + 16 * i:80 + 16 * i])
            near[i, :, cols] = (acc_r[16 * i:16 * i + 16] * SHEAR + part) * KELVIN
        return carry

    lax.fori_loop(0, nl, near_leaf, 0)

    q_row = lax.broadcasted_iota(jnp.int32, (per_row * 16, rows), 0).astype(F32)

    def sum_of(group):
        total = jnp.zeros((per_row * 16, rank), F32)
        for u in range(4):
            block = got[group * 4 + u]
            tag = block[used // 16 * 16:].astype(F32)[used % 16:used % 16 + 1, :rows]
            pick = jnp.where(q_row == tag, 1.0, 0.0).astype(BF16)
            total += dot(pick, block)
        return total

    for u in range(1, 4):
        far_copy(u).wait()
    inc[...] = sum_of(0)

    def collect(group, carry):
        for u in range(4):
            far_copy(group * 4 + u).wait()
        inc[...] += sum_of(group)
        return carry

    lax.fori_loop(1, ndev // 4, collect, 0)

    w[per_row - 1] = inc[(per_row - 1) * 16:per_row * 16].astype(BF16)
    upper = per_row - 1
    for mats, count in ((ut_v, nl // 4), (um_v, nl // 2), (ul_v, nl)):
        lower = upper - count
        for k in range(count):
            q = lower + k
            w[q] = (inc[q * 16:(q + 1) * 16] + dot(w[upper + k // 2], mats[k])).astype(BF16)
        upper = lower
    for t in range(nl):
        for i in range(3):
            out[i, :, t * leaf:(t + 1) * leaf] = near[i, :, t * leaf:(t + 1) * leaf] + dot(w[t], bas_v[t, i])


def body(loads, centers, basis, up_leaf, up_mid, up_top, couplings, far_dest, far_target, near_src):
    cases = loads.shape[0]
    nl, rank, _, leaf = basis.shape
    nsub = lax.axis_size("sub")
    ndev = lax.axis_size("clus") * nsub
    per_row, fan = far_dest.shape
    cap = max(2, (per_row * fan + ndev - 1) // ndev)
    rows = (cap * 12 + 16) // 16 * 16
    width = nl * leaf
    pack = jnp.concatenate([
        jnp.transpose(loads, (1, 0, 2)).reshape(3 * cases, width), centers, jnp.zeros((9, width), BF16)
    ], axis=0)
    dims = (ndev, nsub, cap, nl, fan, rank, leaf)
    hbm = pl.BlockSpec(memory_space=pltpu.HBM)
    vmem = pl.BlockSpec(memory_space=pltpu.VMEM)
    out = pl.pallas_call(
        functools.partial(kernel, dims),
        out_shape=jax.ShapeDtypeStruct((3, 16, width), F32),
        in_specs=[hbm] * 9,
        out_specs=vmem,
        scratch_shapes=[
            pltpu.VMEM(far_dest.shape, jnp.int32),
            pltpu.VMEM(far_target.shape, jnp.int32),
            pltpu.SMEM(near_src.shape, jnp.int32),
            pltpu.VMEM((3, 48, width), BF16),
            pltpu.VMEM((nl, 3, rank, leaf), BF16),
            pltpu.VMEM((nl, rank, rank), BF16),
            pltpu.VMEM((nl // 2, rank, rank), BF16),
            pltpu.VMEM((nl // 4, rank, rank), BF16),
            pltpu.VMEM((per_row * fan, rank, rank), BF16),
            pltpu.VMEM((per_row, 16, rank), BF16),
            pltpu.VMEM((ndev, 128), F32),
            pltpu.VMEM((ndev, 128), jnp.int32),
            pltpu.SMEM((ndev, 128), jnp.int32),
            pltpu.VMEM((ndev, rows, rank), BF16),
            pltpu.VMEM((ndev, rows, rank), BF16),
            pltpu.VMEM((3 * nl, 3, 112, leaf), BF16),
            pltpu.VMEM((3 * nl, 48, leaf), BF16),
            pltpu.VMEM((3 * nl, leaf, 16), F32),
            pltpu.VMEM((2, 4, leaf, leaf), BF16),
            pltpu.VMEM((3, 16, width), F32),
            pltpu.VMEM((per_row * 16, rank), F32),
            pltpu.VMEM((per_row, 16, rank), BF16),
            pltpu.SemaphoreType.DMA((10,)),
            pltpu.SemaphoreType.DMA((2,)),
            pltpu.SemaphoreType.DMA((2,)),
            pltpu.SemaphoreType.DMA((ndev,)),
            pltpu.SemaphoreType.DMA((ndev,)),
        ],
        compiler_params=pltpu.CompilerParams(
            collective_id=0, has_side_effects=True, vmem_limit_bytes=50 * 1024 * 1024
        ),
    )(pack, jnp.transpose(basis, (0, 2, 1, 3)), up_leaf, up_mid, up_top,
      couplings.reshape(per_row * fan, rank, rank), far_dest, far_target, near_src)
    return jnp.transpose(out[:, :cases], (1, 0, 2))


def solution(mesh):
    every = ("groups", "clus", "sub")
    return jax.shard_map(
        body,
        mesh=mesh,
        in_specs=(
            P(None, None, every),
            P(None, every),
            P(every, None, None, None),
            P(every, None, None),
            P(every, None, None),
            P(every, None, None),
            P(every, None, None, None),
            P(every, None),
            P(every, None),
            P(every, None),
        ),
        out_specs=P(None, None, every),
        check_vma=False,
    )
```

time: 60.8 us -> 50.2 us (0.83)
  Pallas kernels: 51.6 us -> 40.8 us
    pallas_call x1, Pallas kernels: 51.6 us -> 40.8 us  [body(): pl.pallas_call(functools.partial(kernel, dims), out_shape=jax.ShapeDtypeS...]
    unnamed x15 -> x14, local copies, waits for them, and re-layouts: 7 us -> 5.96 us
    transpose x0 -> x1, local copies, waits for them, and re-layouts: none -> 1.04 us  [body(): jnp.transpose(loads, (1, 0, 2)).reshape(3 * cases, width)]
where the time goes in v2:
time: 50.2 us; the launch traced here: 49.7 us
  Pallas kernels  40.8 us (81%)
  local copies, waits for them, and re-layouts  8.09 us (16%)
  other arithmetic  0.82 us (2%)
    pallas_call x1, Pallas kernels, body(): pl.pallas_call(functools.partial(kernel, dims), out_shape=jax.ShapeDtypeS...  40.8 us
    unnamed x14, local copies, waits for them, and re-layouts  5.96 us
    transpose x1, local copies, waits for them, and re-layouts, body(): jnp.transpose(loads, (1, 0, 2)).reshape(3 * cases, width)  1.04 us

profile of v2, /device:TPU:0, one launch (start us, length us, event | category | flops | bytes accessed | tf_op | source)
XLA Modules:
  0.0 49.7 jit_solution(14063512265740109902)
XLA Ops:
  0.0 0.1 pad.2.clone
  0.1 1.0 %copy.11 = bf16[3,12,2048]{2,1,0:T(8,128)(2,1)S(1)} copy(bf16[3,12,2048]{2,0,1:T(4,128)(2,1)} %bitcast.7) | data formatting | bytes 294912 | tf_op jit(solution)/shard_map/transpose | solution.py:268
  1.2 0.8 %maximum_maximum_fusion.pack = bf16[48,2048]{1,0:T(8,128)(2,1)S(1)} fusion(bf16[3,2048]{1,0:T(4,128)(2,1)} %param.11, bf16[36,2048]{1,0:T(8,128)(2,1)S(1)} %reshape.6, bf16[48]{0:T(256)(128)(2,1)S(1)} %pad.2.clone), kind=kLoop, calls=%fused_computation.1 | loop fusion | flops 589824 | bytes 356448 | tf_op jit(solution)/shard_map/concatenate | solution.py:267
  2.0 0.0 copy-start
  2.0 1.3 %copy-done = bf16[8,96,3,256]{3,1,2,0:T(8,128)(2,1)S(1)} copy-done((bf16[8,96,3,256]{3,1,2,0:T(8,128)(2,1)S(1)}, bf16[8,96,3,256]{3,1,2,0:T(8,128)(2,1)}, u32[]{:S(2)}) %copy-start) | copy-done | bytes 1179672
  3.3 0.0 copy-start.1
  3.3 0.9 %copy-done.1 = bf16[8,96,96]{2,1,0:T(8,128)(2,1)S(1)} copy-done((bf16[8,96,96]{2,1,0:T(8,128)(2,1)S(1)}, bf16[8,96,96]{2,1,0:T(8,128)(2,1)}, u32[]{:S(2)}) %copy-start.1) | copy-done | bytes 147480
  4.2 0.0 copy-start.2
  4.2 0.9 %copy-done.2 = bf16[4,96,96]{2,1,0:T(8,128)(2,1)S(1)} copy-done((bf16[4,96,96]{2,1,0:T(8,128)(2,1)S(1)}, bf16[4,96,96]{2,1,0:T(8,128)(2,1)}, u32[]{:S(2)}) %copy-start.2) | copy-done | bytes 73752
  5.1 0.0 copy-start.3
  5.1 0.8 %copy-done.3 = bf16[2,96,96]{2,1,0:T(8,128)(2,1)S(1)} copy-done((bf16[2,96,96]{2,1,0:T(8,128)(2,1)S(1)}, bf16[2,96,96]{2,1,0:T(8,128)(2,1)}, u32[]{:S(2)}) %copy-start.3) | copy-done | bytes 36888
  5.9 0.0 copy-start.4
  5.9 0.7 %copy-done.4 = s32[15,12]{1,0:T(8,128)S(1)} copy-done((s32[15,12]{1,0:T(8,128)S(1)}, s32[15,12]{1,0:T(8,128)}, u32[]{:S(2)}) %copy-start.4) | copy-done | bytes 744
  6.6 0.0 copy-start.5
  6.6 0.7 %copy-done.5 = s32[15,12]{1,0:T(8,128)S(1)} copy-done((s32[15,12]{1,0:T(8,128)S(1)}, s32[15,12]{1,0:T(8,128)}, u32[]{:S(2)}) %copy-start.5) | copy-done | bytes 744
  7.3 0.0 copy-start.6
  7.3 0.7 %copy-done.6 = s32[8,6]{1,0:T(8,128)S(1)} copy-done((s32[8,6]{1,0:T(8,128)S(1)}, s32[8,6]{1,0:T(8,128)}, u32[]{:S(2)}) %copy-start.6) | copy-done | bytes 216
  8.0 40.8 %shard_map.100 = f32[3,16,2048]{2,1,0:T(8,128)S(1)} custom-call(bf16[48,2048]{1,0:T(8,128)(2,1)S(1)} %maximum_maximum_fusion.pack, bf16[8,3,96,256]{3,2,1,0:T(8,128)(2,1)S(1)} %bitcast.5, bf16[8,96,96]{2,1,0:T(8,128)(2,1)S(1)} %copy-done.1, bf16[4,96,96]{2,1,0:T(8,128)(2,1)S(1)} %copy-done.2, bf16[2,96,96]{2,1,0:T(8,128)(2,1)S(1)} %copy-done.3, ...), custom_call_target="tpu_custom_call" | custom-call | tf_op jit(solution)/shard_map/pallas_call | solution.py:273
  48.8 0.9 %copy.12 = f32[12,3,2048]{2,1,0:T(4,128)} copy(f32[12,3,2048]{2,0,1:T(8,128)S(1)} %slice_bitcast_fusion) | data formatting | bytes 589824 | tf_op jit(solution)/shard_map/transpose | solution.py:312
  (3 shorter events, 0.1 us)
Async XLA Ops:
  2.0 1.3 %copy-start = (bf16[8,96,3,256]{3,1,2,0:T(8,128)(2,1)S(1)}, bf16[8,96,3,256]{3,1,2,0:T(8,128)(2,1)}, u32[]{:S(2)}) copy-start(bf16[8,96,3,256]{3,1,2,0:T(8,128)(2,1)} %param.12) | copy-start | bytes 3538948
  3.3 0.9 %copy-start.1 = (bf16[8,96,96]{2,1,0:T(8,128)(2,1)S(1)}, bf16[8,96,96]{2,1,0:T(8,128)(2,1)}, u32[]{:S(2)}) copy-start(bf16[8,96,96]{2,1,0:T(8,128)(2,1)} %up_leaf.1) | copy-start | bytes 442372
  4.2 0.9 %copy-start.2 = (bf16[4,96,96]{2,1,0:T(8,128)(2,1)S(1)}, bf16[4,96,96]{2,1,0:T(8,128)(2,1)}, u32[]{:S(2)}) copy-start(bf16[4,96,96]{2,1,0:T(8,128)(2,1)} %up_mid.1) | copy-start | bytes 221188
  5.1 0.8 %copy-start.3 = (bf16[2,96,96]{2,1,0:T(8,128)(2,1)S(1)}, bf16[2,96,96]{2,1,0:T(8,128)(2,1)}, u32[]{:S(2)}) copy-start(bf16[2,96,96]{2,1,0:T(8,128)(2,1)} %up_top.1) | copy-start | bytes 110596
  5.9 0.7 %copy-start.4 = (s32[15,12]{1,0:T(8,128)S(1)}, s32[15,12]{1,0:T(8,128)}, u32[]{:S(2)}) copy-start(s32[15,12]{1,0:T(8,128)} %dest_h.1) | copy-start | bytes 2164
  6.6 0.7 %copy-start.5 = (s32[15,12]{1,0:T(8,128)S(1)}, s32[15,12]{1,0:T(8,128)}, u32[]{:S(2)}) copy-start(s32[15,12]{1,0:T(8,128)} %target_h.1) | copy-start | bytes 2164
  7.3 0.7 %copy-start.6 = (s32[8,6]{1,0:T(8,128)S(1)}, s32[8,6]{1,0:T(8,128)}, u32[]{:S(2)}) copy-start(s32[8,6]{1,0:T(8,128)} %near_h.1) | copy-start | bytes 580
